TPU v7x, 256 devices: a whole 4x4x8 slice. The times are simulated.
256 devices in a mesh: blk: 32 (over y_hi, z, core), head: 8 (over x, y_lo).
Axes of the slice: x: 4, y: 4 (y_hi: 2, y_lo: 2; y = y_hi * 2 + y_lo), z: 8, core: 2. Of those that a mesh axis runs over, the one named last changes fastest.
Arguments:
- queries: bfloat16 [4096, 32, 128], P('blk', 'head'), may hold values from -6 to 6
- keys: bfloat16 [4096, 32, 128], P('blk', 'head'), may hold values from -6 to 6
- values: bfloat16 [4096, 32, 128], P('blk', 'head'), may hold values from -6 to 6
- outputs: bfloat16 [4096, 32, 128], P('blk', 'head'), may hold values from -4 to 4
- lse: float32 [32, 4096], P('head', 'blk')
- positions: int32 [4096], P('blk'), may hold values from 0 to 4095, as said below
- w_out: bfloat16 [4096, 4096], P('head'), may hold values from -0.09375 to 0.09375
- d_layer: bfloat16 [4096, 4096], P('blk', 'head'), may hold values from -6 to 6
Outputs:
- d_queries: bfloat16 [4096, 32, 128], P('blk', 'head')
- d_keys: bfloat16 [4096, 32, 128], P('blk', 'head')
- d_values: bfloat16 [4096, 32, 128], P('blk', 'head')
Inputs may be any that keep to these rules, and one draw needn't show every extreme that they name: A permutation of the positions; each index of blk holds 128 consecutive positions in rising order.
All inputs are finite; a program needn't handle non-finite values.
Results may differ from a plain program's by a relative error of at most 0.006.
Values may be sent and summed in bfloat16 or wider, within the bound.
A program may use at most 128 MiB of HBM per device.

v0:
```python
import functools
import math

import jax
import jax.numpy as jnp
from jax import lax
from jax.experimental import pallas as pl
from jax.experimental.pallas import tpu as pltpu
from jax.sharding import PartitionSpec as P

MESH = pl.DeviceIdType.MESH
BF = jnp.bfloat16
F32 = jnp.float32
LOG2E = 1.0 / math.log(2.0)
SCALE = 1.0 / math.sqrt(128.0)
KV_ROWS = 272
QA_ROWS = 144
VMEM_BYTES = 63 * 1024 * 1024
NT = (((1,), (1,)), ((), ()))
TN = (((0,), (0,)), ((), ()))
NN = (((1,), (0,)), ((), ()))


def dot(a, b, dims):
    return lax.dot_general(a, b, dims, preferred_element_type=F32)


def thirds(value):
    high = value.astype(BF)
    rest = value - high.astype(F32)
    middle = rest.astype(BF)
    low = (rest - middle.astype(F32)).astype(BF)
    return high, middle, low


def kernel(
    dl, w_hbm, v_hbm, k_hbm, q_hbm, o_hbm, lse_ref, pos_ref, out,
    raw, dl_v, gath, w_v, kv_st, qa_st, kv, qa, late, late_out, k_t, dq_acc, dk_acc, dv_acc,
    sq, rq, skv, rkv, fq, fkv, send, recv, local,
):
    b = lax.axis_index("blk")
    hd = lax.axis_index("head")
    yh, z, c = b // 16, (b // 2) % 8, b % 2
    m = z // 2
    sg = 2 * (z % 2) - 1
    x, yl = hd // 2, hd % 2

    def at_z(by):
        return {"blk": yh * 16 + ((z + by + 8) % 8) * 2 + c}

    sibling = {"blk": yh * 16 + z * 2 + (1 - c)}
    across = {"blk": (1 - yh) * 16 + z * 2 + c}
    zpart = at_z(-sg)
    to_z = (None, at_z(sg), at_z(-2 * sg), at_z(3 * sg))
    from_z = (None, at_z(sg), at_z(2 * sg), at_z(3 * sg))
    head_of = (m, (m + sg + 4) % 4, (m - sg + 4) % 4, (m + 2) % 4)
    beside = {"head": x * 2 + (1 - yl)}
    right = {"head": ((x + 1) % 4) * 2 + yl}
    left = {"head": ((x + 3) % 4) * 2 + yl}

    count = [0]
    started = []

    def remote(src, dst, device):
        k = count[0]
        count[0] = k + 1
        return pltpu.make_async_remote_copy(
            src_ref=src, dst_ref=dst, send_sem=send.at[k], recv_sem=recv.at[k],
            device_id=device, device_id_type=MESH,
        )

    def go(copy):
        copy.start()
        started.append(copy)

    raw_copies = [pltpu.make_async_copy(a, raw.at[i], local.at[8 + i]) for i, a in enumerate((v_hbm, k_hbm, q_hbm, o_hbm))]
    dl_copy = pltpu.make_async_copy(dl, dl_v, local.at[12])
    w_copies = []
    for r in range(8):
        dx, dy = r // 2, r % 2
        col = (((x + dx) % 4) * 2 + (yl + dy) % 2) * 512
        w_copies.append(
            pltpu.make_async_copy(w_hbm.at[:, pl.ds(pl.multiple_of(col, 512), 512)], w_v.at[r], local.at[r])
        )
    for copy in raw_copies[:3] + [dl_copy]:
        copy.start()

    barrier = pltpu.get_barrier_semaphore()
    partners = (beside, right, left, sibling, across, zpart, at_z(sg), at_z(-2 * sg), at_z(2 * sg), at_z(3 * sg))
    for device in partners:
        pl.semaphore_signal(barrier, inc=1, device_id=device, device_id_type=MESH)

    rank = jnp.broadcast_to((pos_ref[...] // 128).astype(F32)[:, 0:1], (1, 128))
    aux = []
    for h in range(4):
        parts = thirds(lse_ref[pl.ds(h, 1), :])
        rows = [rank] + [part.astype(F32) for part in parts] + [jnp.zeros((12, 128), F32)]
        aux.append(jnp.concatenate(rows, axis=0).astype(BF))

    def relay_out(i):
        raw_copies[i].wait()
        return jnp.transpose(raw[i].astype(F32), (1, 0, 2)).astype(BF)

    pl.semaphore_wait(barrier, len(partners))

    halves = (pl.ds(0, 64), pl.ds(64, 64))
    g_side = [remote(dl.at[r], gath.at[1, r], beside) for r in halves]
    g_r0 = [remote(dl.at[r], gath.at[6, r], right) for r in halves]
    g_l0 = [remote(dl.at[r], gath.at[2, r], left) for r in halves]
    g_r1 = [remote(gath.at[1, r], gath.at[7, r], right) for r in halves]
    g_l1 = [remote(gath.at[1, r], gath.at[3, r], left) for r in halves]
    g_r2 = remote(gath.at[6, halves[0]], gath.at[4, halves[0]], right)
    g_l2 = remote(gath.at[2, halves[1]], gath.at[4, halves[1]], left)
    g_r3 = remote(gath.at[7, halves[0]], gath.at[5, halves[0]], right)
    g_l3 = remote(gath.at[3, halves[1]], gath.at[5, halves[1]], left)
    for copy in (g_side[0], g_r0[0], g_l0[1], g_side[1], g_r0[1], g_l0[0]):
        go(copy)

    kv_st[:, pl.ds(0, 128), :] = relay_out(0)
    kv_st[:, pl.ds(128, 128), :] = relay_out(1)
    for h in range(4):
        kv_st[h, pl.ds(256, 16), :] = aux[h]
        qa_st[h, pl.ds(0, 16), :] = aux[h]
    kv_z = [None] + [remote(kv_st.at[head_of[d]], kv.at[0, d], to_z[d]) for d in (1, 2, 3)]
    qa_z = [None] + [remote(qa_st.at[head_of[d]], qa.at[0, d], to_z[d]) for d in (1, 2, 3)]
    qa_sib = [remote(qa_st.at[m] if d == 0 else qa.at[0, d], qa.at[1, d], sibling) for d in range(4)]
    qa_zp = [remote(qa_st.at[m] if d == 0 else qa.at[0, d], qa.at[2, d], zpart) for d in range(4)]
    qa_fwd = [remote(qa.at[2, d], qa.at[3, d], sibling) for d in range(4)]
    kv_y = [remote(kv_st.at[m] if d == 0 else kv.at[0, d], kv.at[1, d], across) for d in range(4)]
    for d in (3, 2, 1):
        go(kv_z[d])
    go(kv_y[0])
    for copy in (raw_copies[3], *(w_copies[r] for r in (0, 1, 6, 2, 7, 3, 4, 5))):
        copy.start()
    qa_st[:, pl.ds(16, 128), :] = relay_out(2)
    for d in (3, 2, 1):
        go(qa_z[d])
    go(qa_zp[0])
    go(qa_sib[0])
    kv[0, 0] = kv_st[m]
    qa[0, 0] = qa_st[m]

    def project(r):
        w_copies[r].wait()
        shard = dl_v[...] if r == 0 else gath[r]
        return dot(shard, w_v[r], NT)

    g_side[0].wait_recv()
    go(g_r1[0])
    go(g_l1[0])
    g_r0[0].wait_recv()
    go(g_r2)
    g_l0[1].wait_recv()
    go(g_l2)
    g_side[1].wait_recv()
    go(g_l1[1])
    go(g_r1[1])
    o_heads = relay_out(3)
    dl_copy.wait()
    total = project(0)
    total += project(1)
    g_r1[0].wait_recv()
    go(g_r3)
    g_l1[1].wait_recv()
    go(g_l3)
    g_r0[1].wait_recv()
    total += project(6)
    g_l0[0].wait_recv()
    total += project(2)
    g_r1[1].wait_recv()
    total += project(7)
    g_l1[0].wait_recv()
    total += project(3)
    for d in (1, 2, 3):
        kv_z[d].wait_recv()
        go(kv_y[d])
        qa_z[d].wait_recv()
        go(qa_zp[d])
        go(qa_sib[d])
    g_r2.wait_recv()
    g_l2.wait_recv()
    total += project(4)
    g_r3.wait_recv()
    g_l3.wait_recv()
    total += project(5)

    for h in range(4):
        part = total[:, h * 128:(h + 1) * 128].astype(BF)
        late_out[h, pl.ds(0, 128), :] = part
        col = jnp.sum(part.astype(F32) * o_heads[h].astype(F32), axis=1, keepdims=True)
        row = jnp.transpose(jnp.broadcast_to(col, (128, 128)))[0:1, :]
        rows = [part.astype(F32) for part in thirds(row)] + [jnp.zeros((13, 128), F32)]
        late_out[h, pl.ds(128, 16), :] = jnp.concatenate(rows, axis=0).astype(BF)

    late_z = [None] + [remote(late_out.at[head_of[d]], late.at[0, d], to_z[d]) for d in (1, 2, 3)]
    late_sib = [remote(late_out.at[m] if d == 0 else late.at[0, d], late.at[1, d], sibling) for d in range(4)]
    late_zp = [remote(late_out.at[m] if d == 0 else late.at[0, d], late.at[2, d], zpart) for d in range(4)]
    late_fwd = [remote(late.at[2, d], late.at[3, d], sibling) for d in range(4)]
    for d in (3, 2, 1):
        go(late_z[d])
    go(late_zp[0])
    go(late_sib[0])
    late[0, 0] = late_out[m]
    for d in range(4):
        qa_zp[d].wait_recv()
        go(qa_fwd[d])
    for d in range(4):
        k_t[0, :, pl.ds(d * 128, 128)] = jnp.transpose(kv[0, d, pl.ds(128, 128), :].astype(F32)).astype(BF)
    for d in range(4):
        kv_y[d].wait_recv()
        k_t[1, :, pl.ds(d * 128, 128)] = jnp.transpose(kv[1, d, pl.ds(128, 128), :].astype(F32)).astype(BF)
    for d in (1, 2, 3):
        late_z[d].wait_recv()
        go(late_zp[d])
        go(late_sib[d])

    def step(kk, kp, qc, first_k=False, first_q=False):
        keys = [kv[kk, 2 * kp + i, pl.ds(128, 128), :] for i in (0, 1)]
        k = jnp.concatenate(keys, axis=0)
        v = jnp.concatenate([kv[kk, 2 * kp + i, pl.ds(0, 128), :] for i in (0, 1)], axis=0)
        q = jnp.concatenate([qa[qc, i, pl.ds(16, 128), :] for i in range(4)], axis=0)
        do = jnp.concatenate([late[qc, i, pl.ds(0, 128), :] for i in range(4)], axis=0)
        aux = jnp.concatenate([qa[qc, i, pl.ds(0, 16), :].astype(F32) for i in range(4)], axis=1)
        aux2 = jnp.concatenate([late[qc, i, pl.ds(128, 16), :].astype(F32) for i in range(4)], axis=1)
        q_rank = aux[0:1]
        lse = (aux[1:2] + aux[2:3] + aux[3:4]) * LOG2E
        delta = aux2[0:1] + aux2[1:2] + aux2[2:3]
        scores = dot(k, q, NT)
        d_probs = dot(v, do, NT)
        parts = []
        for i in (0, 1):
            k_rank = kv[kk, 2 * kp + i, pl.ds(256, 16), :].astype(F32)[0:1]
            k_rank = jnp.concatenate([k_rank] * 4, axis=1)
            shift = jnp.where(k_rank <= q_rank, lse, jnp.inf)
            parts.append(scores[i * 128:(i + 1) * 128] * (SCALE * LOG2E) - shift)
        exponent = jnp.concatenate(parts, axis=0)
        if kk == 0 and qc == 0:
            row = lax.broadcasted_iota(jnp.int32, (256, 512), 0) + kp * 256
            col = lax.broadcasted_iota(jnp.int32, (256, 512), 1)
            seen = (row <= col) | (row // 128 != col // 128)
            exponent = jnp.where(seen, exponent, -jnp.inf)
        probs = jnp.exp2(exponent)
        probs_b = probs.astype(BF)
        d_scores = (probs * (d_probs - delta)).astype(BF)
        rows = pl.ds(kp * 256, 256)
        d_v = dot(probs_b, do, NN)
        d_k = dot(d_scores, q, NN)
        d_q = dot(k_t[kk, :, rows], d_scores, NN)
        dv_acc[kk, rows, :] = d_v if first_k else dv_acc[kk, rows, :] + d_v
        dk_acc[kk, rows, :] = d_k if first_k else dk_acc[kk, rows, :] + d_k
        dq_acc[qc] = d_q if first_q else dq_acc[qc] + d_q

    step(1, 1, 0, True, True)
    step(1, 0, 0, True)
    for d in range(4):
        late_zp[d].wait_recv()
        go(late_fwd[d])
    step(0, 1, 0, True)
    step(0, 0, 0, True)
    for d in range(4):
        qa_sib[d].wait_recv()
        late_sib[d].wait_recv()
    step(1, 1, 1, False, True)
    step(1, 0, 1)
    step(1, 1, 2, False, True)
    step(1, 0, 2)
    for d in range(4):
        qa_fwd[d].wait_recv()
        late_fwd[d].wait_recv()
    kv_back = [remote(skv.at[d], rkv.at[d], across) for d in range(4)]
    for kp in (1, 0):
        step(1, kp, 3, False, kp == 1)
        for d in (2 * kp + 1, 2 * kp):
            rows = pl.ds(d * 128, 128)
            skv[d, pl.ds(0, 128), :] = dv_acc[1, rows, :].astype(BF)
            skv[d, pl.ds(128, 128), :] = (dk_acc[1, rows, :] * SCALE).astype(BF)
            go(kv_back[d])

    step(0, 1, 3)
    step(0, 0, 3)
    sq[0] = (dq_acc[3] * SCALE).astype(BF)
    q_back3 = remote(sq.at[0], rq.at[0], sibling)
    go(q_back3)
    step(0, 1, 2)
    step(0, 0, 2)
    q_back3.wait_recv()
    sq[1] = (dq_acc[2] * SCALE + rq[0].astype(F32)).astype(BF)
    q_back2 = remote(sq.at[1], rq.at[1], zpart)
    go(q_back2)
    step(0, 1, 1)
    step(0, 0, 1)
    sq[2] = (dq_acc[1] * SCALE).astype(BF)
    q_back1 = remote(sq.at[2], rq.at[2], sibling)
    go(q_back1)

    out_kv = [None] + [remote(fkv.at[d], out.at[m, pl.ds(128, 256)], from_z[d]) for d in (1, 2, 3)]
    out_q = [None] + [remote(fq.at[d], out.at[m, pl.ds(0, 128)], from_z[d]) for d in (1, 2, 3)]
    for d in (3, 2, 1, 0):
        rows = pl.ds(d * 128, 128)
        kv_back[d].wait_recv()
        fkv[d, pl.ds(0, 128), :] = (dv_acc[0, rows, :] + rkv[d, pl.ds(0, 128), :].astype(F32)).astype(BF)
        fkv[d, pl.ds(128, 128), :] = (
            dk_acc[0, rows, :] * SCALE + rkv[d, pl.ds(128, 128), :].astype(F32)
        ).astype(BF)
        if d > 0:
            go(out_kv[d])
    keep_kv = pltpu.make_async_copy(fkv.at[0], out.at[m, pl.ds(128, 256)], local.at[14])
    keep_kv.start()
    q_back1.wait_recv()
    q_back2.wait_recv()
    for d in (3, 2, 1, 0):
        rows = pl.ds(d * 128, 128)
        summed = dq_acc[0, :, rows] * SCALE + (rq[1, :, rows].astype(F32) + rq[2, :, rows].astype(F32))
        fq[d] = jnp.transpose(summed).astype(BF)
        if d > 0:
            go(out_q[d])
    keep_q = pltpu.make_async_copy(fq.at[0], out.at[m, pl.ds(0, 128)], local.at[13])
    keep_q.start()
    keep_kv.wait()
    keep_q.wait()
    for d in (1, 2, 3):
        out_kv[d].wait_recv()
        out_q[d].wait_recv()
    for copy in started:
        copy.wait_send()


COPIES = 80


def token_major(blocks, d_q, d_k, d_v, held, turned, sem):
    outs = ((0, d_q), (2, d_k), (1, d_v))
    loads = [pltpu.make_async_copy(blocks.at[:, pl.ds(128 * i, 128)], held.at[i], sem.at[i]) for i, _ in outs]
    stores = [pltpu.make_async_copy(turned.at[i], out, sem.at[3 + i]) for i, out in outs]
    for load in loads:
        load.start()
    for (i, _), load, store in zip(outs, loads, stores):
        load.wait()
        turned[i] = jnp.transpose(held[i].astype(F32), (1, 0, 2)).astype(BF)
        store.start()
    for store in stores:
        store.wait()


def on_device(queries, keys, values, outputs, lse, positions, w_out, d_layer):
    vmem = pl.BlockSpec(memory_space=pltpu.VMEM)
    hbm = pl.BlockSpec(memory_space=pl.ANY)
    grads = pl.pallas_call(
        kernel,
        out_shape=jax.ShapeDtypeStruct((4, 384, 128), BF),
        in_specs=[hbm] * 6 + [vmem] * 2,
        out_specs=hbm,
        scratch_shapes=[
            pltpu.VMEM((4, 128, 4, 128), BF),
            pltpu.VMEM((128, 512), BF),
            pltpu.VMEM((8, 128, 512), BF),
            pltpu.VMEM((8, 512, 512), BF),
            pltpu.VMEM((4, KV_ROWS, 128), BF),
            pltpu.VMEM((4, QA_ROWS, 128), BF),
            pltpu.VMEM((2, 4, KV_ROWS, 128), BF),
            pltpu.VMEM((4, 4, QA_ROWS, 128), BF),
            pltpu.VMEM((4, 4, QA_ROWS, 128), BF),
            pltpu.VMEM((4, QA_ROWS, 128), BF),
            pltpu.VMEM((2, 128, 512), BF),
            pltpu.VMEM((4, 128, 512), F32),
            pltpu.VMEM((2, 512, 128), F32),
            pltpu.VMEM((2, 512, 128), F32),
            pltpu.VMEM((3, 128, 512), BF),
            pltpu.VMEM((3, 128, 512), BF),
            pltpu.VMEM((4, 256, 128), BF),
            pltpu.VMEM((4, 256, 128), BF),
            pltpu.VMEM((4, 128, 128), BF),
            pltpu.VMEM((4, 256, 128), BF),
            pltpu.SemaphoreType.DMA((COPIES,)),
            pltpu.SemaphoreType.DMA((COPIES,)),
            pltpu.SemaphoreType.DMA((16,)),
        ],
        compiler_params=pltpu.CompilerParams(
            collective_id=0, has_side_effects=True, vmem_limit_bytes=VMEM_BYTES
        ),
    )(d_layer, w_out, values, keys, queries, outputs, lse, positions.reshape(1, 128))
    return pl.pallas_call(
        token_major,
        out_shape=[jax.ShapeDtypeStruct((128, 4, 128), BF)] * 3,
        in_specs=[hbm],
        out_specs=[hbm] * 3,
        scratch_shapes=[
            pltpu.VMEM((3, 4, 128, 128), BF),
            pltpu.VMEM((3, 128, 4, 128), BF),
            pltpu.SemaphoreType.DMA((6,)),
        ],
        compiler_params=pltpu.CompilerParams(vmem_limit_bytes=VMEM_BYTES),
    )(grads)


def solution(mesh):
    in_specs = (
        P("blk", "head", None),
        P("blk", "head", None),
        P("blk", "head", None),
        P("blk", "head", None),
        P("head", "blk"),
        P("blk"),
        P("head", None),
        P("blk", "head"),
    )
    out_specs = (P("blk", "head", None), P("blk", "head", None), P("blk", "head", None))
    return jax.shard_map(
        on_device, mesh=mesh, in_specs=in_specs, out_specs=out_specs, check_vma=False
    )
```

profile of v0, /device:TPU:2, one launch (start us, length us, event | category | flops | bytes accessed | tf_op | source)
XLA Modules:
  0.0 51.8 jit_solution(2862441505541576543)
XLA Ops:
  0.6 49.3 %shard_map.103.blocks = bf16[4,384,128]{2,1,0:T(8,128)(2,1)} custom-call(bf16[128,512]{1,0:T(8,128)(2,1)} %dl.1, bf16[512,4096]{1,0:T(8,128)(2,1)} %w_hbm.1, bf16[128,4,128]{2,1,0:T(4,128)(2,1)} %v_hbm.1, bf16[128,4,128]{2,1,0:T(4,128)(2,1)} %k_hbm.1, bf16[128,4,128]{2,1,0:T(4,128)(2,1)} %q_hbm.1, bf16[128,4,128]{2,1,0:T(4,128)(2,1)} %o_hbm.1, ...), custom_call_target="tpu_custom_call" | custom-call | tf_op jit(solution)/shard_map/pallas_call | solution.py:348
  50.0 1.8 %shard_map.104 = (bf16[128,4,128]{2,1,0:T(4,128)(2,1)}, bf16[128,4,128]{2,1,0:T(4,128)(2,1)}, bf16[128,4,128]{2,1,0:T(4,128)(2,1)}) custom-call(bf16[4,384,128]{2,1,0:T(8,128)(2,1)} %shard_map.103.blocks), custom_call_target="tpu_custom_call" | custom-call | tf_op jit(solution)/shard_map/pallas_call | solution.py:382
where the time goes:
time: 51.9 us; the launch traced here: 51.8 us
  Pallas kernels  51.2 us (99%)
  between operations  0.64 us (1%)
    pallas_call x1, Pallas kernels, on_device(): pl.pallas_call(kernel, out_shape=jax.ShapeDtypeStruct((4, 384, 128), BF),...  49.3 us
    pallas_call x1, Pallas kernels, on_device(): pl.pallas_call(token_major, out_shape=[jax.ShapeDtypeStruct((128, 4, 128)...  1.83 us

commit v1 on v0

--- a/solution.py
+++ b/solution.py
@@ -82,7 +82,7 @@
         w_copies.append(
             pltpu.make_async_copy(w_hbm.at[:, pl.ds(pl.multiple_of(col, 512), 512)], w_v.at[r], local.at[r])
         )
-    for copy in raw_copies[:3] + [dl_copy]:
+    for copy in [raw_copies[i] for i in (2, 0, 1)] + [dl_copy, raw_copies[3]] + [w_copies[r] for r in (0, 1, 6, 2, 7, 3, 4, 5)]:
         copy.start()
 
     barrier = pltpu.get_barrier_semaphore()
@@ -116,27 +116,25 @@
     for copy in (g_side[0], g_r0[0], g_l0[1], g_side[1], g_r0[1], g_l0[0]):
         go(copy)
 
-    kv_st[:, pl.ds(0, 128), :] = relay_out(0)
-    kv_st[:, pl.ds(128, 128), :] = relay_out(1)
-    for h in range(4):
-        kv_st[h, pl.ds(256, 16), :] = aux[h]
-        qa_st[h, pl.ds(0, 16), :] = aux[h]
     kv_z = [None] + [remote(kv_st.at[head_of[d]], kv.at[0, d], to_z[d]) for d in (1, 2, 3)]
     qa_z = [None] + [remote(qa_st.at[head_of[d]], qa.at[0, d], to_z[d]) for d in (1, 2, 3)]
     qa_sib = [remote(qa_st.at[m] if d == 0 else qa.at[0, d], qa.at[1, d], sibling) for d in range(4)]
     qa_zp = [remote(qa_st.at[m] if d == 0 else qa.at[0, d], qa.at[2, d], zpart) for d in range(4)]
     qa_fwd = [remote(qa.at[2, d], qa.at[3, d], sibling) for d in range(4)]
     kv_y = [remote(kv_st.at[m] if d == 0 else kv.at[0, d], kv.at[1, d], across) for d in range(4)]
-    for d in (3, 2, 1):
-        go(kv_z[d])
-    go(kv_y[0])
-    for copy in (raw_copies[3], *(w_copies[r] for r in (0, 1, 6, 2, 7, 3, 4, 5))):
-        copy.start()
     qa_st[:, pl.ds(16, 128), :] = relay_out(2)
+    for h in range(4):
+        kv_st[h, pl.ds(256, 16), :] = aux[h]
+        qa_st[h, pl.ds(0, 16), :] = aux[h]
     for d in (3, 2, 1):
         go(qa_z[d])
     go(qa_zp[0])
     go(qa_sib[0])
+    kv_st[:, pl.ds(0, 128), :] = relay_out(0)
+    kv_st[:, pl.ds(128, 128), :] = relay_out(1)
+    for d in (3, 2, 1):
+        go(kv_z[d])
+    go(kv_y[0])
     kv[0, 0] = kv_st[m]
     qa[0, 0] = qa_st[m]
 
@@ -144,6 +142,15 @@
         w_copies[r].wait()
         shard = dl_v[...] if r == 0 else gath[r]
         return dot(shard, w_v[r], NT)
+
+    def pass_keys(d):
+        kv_z[d].wait_recv()
+        go(kv_y[d])
+
+    def pass_queries(d):
+        qa_z[d].wait_recv()
+        go(qa_zp[d])
+        go(qa_sib[d])
 
     g_side[0].wait_recv()
     go(g_r1[0])
@@ -159,27 +166,26 @@
     dl_copy.wait()
     total = project(0)
     total += project(1)
+    pass_queries(3)
     g_r1[0].wait_recv()
     go(g_r3)
     g_l1[1].wait_recv()
     go(g_l3)
+    pass_queries(2)
     g_r0[1].wait_recv()
     total += project(6)
     g_l0[0].wait_recv()
     total += project(2)
+    pass_queries(1)
     g_r1[1].wait_recv()
     total += project(7)
     g_l1[0].wait_recv()
     total += project(3)
-    for d in (1, 2, 3):
-        kv_z[d].wait_recv()
-        go(kv_y[d])
-        qa_z[d].wait_recv()
-        go(qa_zp[d])
-        go(qa_sib[d])
+    pass_keys(3)
     g_r2.wait_recv()
     g_l2.wait_recv()
     total += project(4)
+    pass_keys(2)
     g_r3.wait_recv()
     g_l3.wait_recv()
     total += project(5)
@@ -201,18 +207,19 @@
     go(late_zp[0])
     go(late_sib[0])
     late[0, 0] = late_out[m]
-    for d in range(4):
+    pass_keys(1)
+    for d in (0, 3, 2, 1):
         qa_zp[d].wait_recv()
         go(qa_fwd[d])
+    for d in (3, 2, 1):
+        late_z[d].wait_recv()
+        go(late_zp[d])
+        go(late_sib[d])
     for d in range(4):
         k_t[0, :, pl.ds(d * 128, 128)] = jnp.transpose(kv[0, d, pl.ds(128, 128), :].astype(F32)).astype(BF)
     for d in range(4):
         kv_y[d].wait_recv()
         k_t[1, :, pl.ds(d * 128, 128)] = jnp.transpose(kv[1, d, pl.ds(128, 128), :].astype(F32)).astype(BF)
-    for d in (1, 2, 3):
-        late_z[d].wait_recv()
-        go(late_zp[d])
-        go(late_sib[d])
 
     def step(kk, kp, qc, first_k=False, first_q=False):
         keys = [kv[kk, 2 * kp + i, pl.ds(128, 128), :] for i in (0, 1)]
@@ -252,7 +259,7 @@
 
     step(1, 1, 0, True, True)
     step(1, 0, 0, True)
-    for d in range(4):
+    for d in (0, 3, 2, 1):
         late_zp[d].wait_recv()
         go(late_fwd[d])
     step(0, 1, 0, True)
@@ -284,9 +291,12 @@
     step(0, 1, 2)
     step(0, 0, 2)
     q_back3.wait_recv()
-    sq[1] = (dq_acc[2] * SCALE + rq[0].astype(F32)).astype(BF)
-    q_back2 = remote(sq.at[1], rq.at[1], zpart)
-    go(q_back2)
+    q_back2 = [None] * 4
+    for d in (3, 2, 1, 0):
+        cols = pl.ds(d * 128, 128)
+        sq[1, :, cols] = (dq_acc[2, :, cols] * SCALE + rq[0, :, cols].astype(F32)).astype(BF)
+        q_back2[d] = remote(sq.at[1, :, cols], rq.at[1, :, cols], zpart)
+        go(q_back2[d])
     step(0, 1, 1)
     step(0, 0, 1)
     sq[2] = (dq_acc[1] * SCALE).astype(BF)
@@ -307,22 +317,22 @@
     keep_kv = pltpu.make_async_copy(fkv.at[0], out.at[m, pl.ds(128, 256)], local.at[14])
     keep_kv.start()
     q_back1.wait_recv()
-    q_back2.wait_recv()
     for d in (3, 2, 1, 0):
         rows = pl.ds(d * 128, 128)
+        q_back2[d].wait_recv()
         summed = dq_acc[0, :, rows] * SCALE + (rq[1, :, rows].astype(F32) + rq[2, :, rows].astype(F32))
         fq[d] = jnp.transpose(summed).astype(BF)
         if d > 0:
             go(out_q[d])
     keep_q = pltpu.make_async_copy(fq.at[0], out.at[m, pl.ds(0, 128)], local.at[13])
     keep_q.start()
-    keep_kv.wait()
-    keep_q.wait()
+    for copy in started:
+        copy.wait_send()
     for d in (1, 2, 3):
         out_kv[d].wait_recv()
         out_q[d].wait_recv()
-    for copy in started:
-        copy.wait_send()
+    keep_kv.wait()
+    keep_q.wait()
 
 
 COPIES = 80

time: 51.9 us -> 51.7 us (level)
  no operation moved by 1% of the time
where the time goes in v1:
time: 51.7 us; the launch traced here: 51.6 us
  Pallas kernels  51 us (99%)
  between operations  0.64 us (1%)
    pallas_call x1, Pallas kernels, on_device(): pl.pallas_call(kernel, out_shape=jax.ShapeDtypeStruct((4, 384, 128), BF),...  49.1 us
    pallas_call x1, Pallas kernels, on_device(): pl.pallas_call(token_major, out_shape=[jax.ShapeDtypeStruct((128, 4, 128)...  1.83 us

profile of v1, /device:TPU:2, one launch (start us, length us, event | category | flops | bytes accessed | tf_op | source)
XLA Modules:
  0.0 51.6 jit_solution(12794719487259576133)
XLA Ops:
  0.6 49.1 %shard_map.103.blocks = bf16[4,384,128]{2,1,0:T(8,128)(2,1)} custom-call(bf16[128,512]{1,0:T(8,128)(2,1)} %dl.1, bf16[512,4096]{1,0:T(8,128)(2,1)} %w_hbm.1, bf16[128,4,128]{2,1,0:T(4,128)(2,1)} %v_hbm.1, bf16[128,4,128]{2,1,0:T(4,128)(2,1)} %k_hbm.1, bf16[128,4,128]{2,1,0:T(4,128)(2,1)} %q_hbm.1, bf16[128,4,128]{2,1,0:T(4,128)(2,1)} %o_hbm.1, ...), custom_call_target="tpu_custom_call" | custom-call | tf_op jit(solution)/shard_map/pallas_call | solution.py:358
  49.8 1.8 %shard_map.104 = (bf16[128,4,128]{2,1,0:T(4,128)(2,1)}, bf16[128,4,128]{2,1,0:T(4,128)(2,1)}, bf16[128,4,128]{2,1,0:T(4,128)(2,1)}) custom-call(bf16[4,384,128]{2,1,0:T(8,128)(2,1)} %shard_map.103.blocks), custom_call_target="tpu_custom_call" | custom-call | tf_op jit(solution)/shard_map/pallas_call | solution.py:392

commit v2 on v1

--- a/solution.py
+++ b/solution.py
@@ -82,7 +82,7 @@
         w_copies.append(
             pltpu.make_async_copy(w_hbm.at[:, pl.ds(pl.multiple_of(col, 512), 512)], w_v.at[r], local.at[r])
         )
-    for copy in [raw_copies[i] for i in (2, 0, 1)] + [dl_copy, raw_copies[3]] + [w_copies[r] for r in (0, 1, 6, 2, 7, 3, 4, 5)]:
+    for copy in [raw_copies[i] for i in (2, 0, 1)] + [dl_copy, raw_copies[3]] + [w_copies[r] for r in (0, 1, 4, 6, 2, 7, 3, 5)]:
         copy.start()
 
     barrier = pltpu.get_barrier_semaphore()
@@ -99,7 +99,7 @@
 
     def relay_out(i):
         raw_copies[i].wait()
-        return jnp.transpose(raw[i].astype(F32), (1, 0, 2)).astype(BF)
+        return jnp.transpose(raw[i], (1, 0, 2))
 
     pl.semaphore_wait(barrier, len(partners))
 
@@ -111,8 +111,7 @@
     g_l1 = [remote(gath.at[1, r], gath.at[3, r], left) for r in halves]
     g_r2 = remote(gath.at[6, halves[0]], gath.at[4, halves[0]], right)
     g_l2 = remote(gath.at[2, halves[1]], gath.at[4, halves[1]], left)
-    g_r3 = remote(gath.at[7, halves[0]], gath.at[5, halves[0]], right)
-    g_l3 = remote(gath.at[3, halves[1]], gath.at[5, halves[1]], left)
+    g_far = [remote(gath.at[4, r], gath.at[5, r], beside) for r in halves]
     for copy in (g_side[0], g_r0[0], g_l0[1], g_side[1], g_r0[1], g_l0[0]):
         go(copy)
 
@@ -134,7 +133,6 @@
     kv_st[:, pl.ds(128, 128), :] = relay_out(1)
     for d in (3, 2, 1):
         go(kv_z[d])
-    go(kv_y[0])
     kv[0, 0] = kv_st[m]
     qa[0, 0] = qa_st[m]
 
@@ -152,13 +150,13 @@
         go(qa_zp[d])
         go(qa_sib[d])
 
-    g_side[0].wait_recv()
-    go(g_r1[0])
-    go(g_l1[0])
     g_r0[0].wait_recv()
     go(g_r2)
     g_l0[1].wait_recv()
     go(g_l2)
+    g_side[0].wait_recv()
+    go(g_r1[0])
+    go(g_l1[0])
     g_side[1].wait_recv()
     go(g_l1[1])
     go(g_r1[1])
@@ -167,28 +165,28 @@
     total = project(0)
     total += project(1)
     pass_queries(3)
-    g_r1[0].wait_recv()
-    go(g_r3)
-    g_l1[1].wait_recv()
-    go(g_l3)
+    g_r2.wait_recv()
+    go(g_far[0])
+    g_l2.wait_recv()
+    go(g_far[1])
     pass_queries(2)
+    go(kv_y[0])
+    total += project(4)
     g_r0[1].wait_recv()
     total += project(6)
     g_l0[0].wait_recv()
     total += project(2)
     pass_queries(1)
-    g_r1[1].wait_recv()
+    for f in (0, 1):
+        g_r1[f].wait_recv()
+        g_l1[f].wait_recv()
     total += project(7)
-    g_l1[0].wait_recv()
     total += project(3)
     pass_keys(3)
-    g_r2.wait_recv()
-    g_l2.wait_recv()
-    total += project(4)
+    g_far[0].wait_recv()
+    g_far[1].wait_recv()
+    total += project(5)
     pass_keys(2)
-    g_r3.wait_recv()
-    g_l3.wait_recv()
-    total += project(5)
 
     for h in range(4):
         part = total[:, h * 128:(h + 1) * 128].astype(BF)
@@ -211,15 +209,19 @@
     for d in (0, 3, 2, 1):
         qa_zp[d].wait_recv()
         go(qa_fwd[d])
+    def turn_across(d):
+        kv_y[d].wait_recv()
+        k_t[1, :, pl.ds(d * 128, 128)] = jnp.transpose(kv[1, d, pl.ds(128, 128), :].astype(F32)).astype(BF)
+
+    for d in range(4):
+        k_t[0, :, pl.ds(d * 128, 128)] = jnp.transpose(kv[0, d, pl.ds(128, 128), :].astype(F32)).astype(BF)
+    for d in (0, 3, 2):
+        turn_across(d)
     for d in (3, 2, 1):
         late_z[d].wait_recv()
         go(late_zp[d])
         go(late_sib[d])
-    for d in range(4):
-        k_t[0, :, pl.ds(d * 128, 128)] = jnp.transpose(kv[0, d, pl.ds(128, 128), :].astype(F32)).astype(BF)
-    for d in range(4):
-        kv_y[d].wait_recv()
-        k_t[1, :, pl.ds(d * 128, 128)] = jnp.transpose(kv[1, d, pl.ds(128, 128), :].astype(F32)).astype(BF)
+    turn_across(1)
 
     def step(kk, kp, qc, first_k=False, first_q=False):
         keys = [kv[kk, 2 * kp + i, pl.ds(128, 128), :] for i in (0, 1)]
@@ -262,8 +264,6 @@
     for d in (0, 3, 2, 1):
         late_zp[d].wait_recv()
         go(late_fwd[d])
-    step(0, 1, 0, True)
-    step(0, 0, 0, True)
     for d in range(4):
         qa_sib[d].wait_recv()
         late_sib[d].wait_recv()
@@ -283,8 +283,8 @@
             skv[d, pl.ds(128, 128), :] = (dk_acc[1, rows, :] * SCALE).astype(BF)
             go(kv_back[d])
 
-    step(0, 1, 3)
-    step(0, 0, 3)
+    step(0, 1, 3, True)
+    step(0, 0, 3, True)
     sq[0] = (dq_acc[3] * SCALE).astype(BF)
     q_back3 = remote(sq.at[0], rq.at[0], sibling)
     go(q_back3)
@@ -302,6 +302,8 @@
     sq[2] = (dq_acc[1] * SCALE).astype(BF)
     q_back1 = remote(sq.at[2], rq.at[2], sibling)
     go(q_back1)
+    step(0, 1, 0)
+    step(0, 0, 0)
 
     out_kv = [None] + [remote(fkv.at[d], out.at[m, pl.ds(128, 256)], from_z[d]) for d in (1, 2, 3)]
     out_q = [None] + [remote(fq.at[d], out.at[m, pl.ds(0, 128)], from_z[d]) for d in (1, 2, 3)]
@@ -346,7 +348,7 @@
         load.start()
     for (i, _), load, store in zip(outs, loads, stores):
         load.wait()
-        turned[i] = jnp.transpose(held[i].astype(F32), (1, 0, 2)).astype(BF)
+        turned[i] = jnp.transpose(held[i], (1, 0, 2))
         store.start()
     for store in stores:
         store.wait()

time: 51.7 us -> 52.8 us (1.021)
  Pallas kernels: 51 us -> 52 us
    pallas_call x1, Pallas kernels: 49.1 us -> 50.2 us  [on_device(): pl.pallas_call(kernel, out_shape=jax.ShapeDtypeStruct((4, 384, 128), BF),...]
where the time goes in v2:
time: 52.8 us; the launch traced here: 52.7 us
  Pallas kernels  52 us (98%)
  between operations  0.64 us (1%)
    pallas_call x1, Pallas kernels, on_device(): pl.pallas_call(kernel, out_shape=jax.ShapeDtypeStruct((4, 384, 128), BF),...  50.2 us
    pallas_call x1, Pallas kernels, on_device(): pl.pallas_call(token_major, out_shape=[jax.ShapeDtypeStruct((128, 4, 128)...  1.8 us

profile of v2, /device:TPU:2, one launch (start us, length us, event | category | flops | bytes accessed | tf_op | source)
XLA Modules:
  0.0 52.7 jit_solution(10978189787154875553)
XLA Ops:
  0.6 50.2 %shard_map.103.blocks = bf16[4,384,128]{2,1,0:T(8,128)(2,1)} custom-call(bf16[128,512]{1,0:T(8,128)(2,1)} %dl.1, bf16[512,4096]{1,0:T(8,128)(2,1)} %w_hbm.1, bf16[128,4,128]{2,1,0:T(4,128)(2,1)} %v_hbm.1, bf16[128,4,128]{2,1,0:T(4,128)(2,1)} %k_hbm.1, bf16[128,4,128]{2,1,0:T(4,128)(2,1)} %q_hbm.1, bf16[128,4,128]{2,1,0:T(4,128)(2,1)} %o_hbm.1, ...), custom_call_target="tpu_custom_call" | custom-call | tf_op jit(solution)/shard_map/pallas_call | solution.py:360
  50.9 1.8 %shard_map.104 = (bf16[128,4,128]{2,1,0:T(4,128)(2,1)}, bf16[128,4,128]{2,1,0:T(4,128)(2,1)}, bf16[128,4,128]{2,1,0:T(4,128)(2,1)}) custom-call(bf16[4,384,128]{2,1,0:T(8,128)(2,1)} %shard_map.103.blocks), custom_call_target="tpu_custom_call" | custom-call | tf_op jit(solution)/shard_map/pallas_call | solution.py:394

commit v3 on v1

--- a/solution.py
+++ b/solution.py
@@ -99,7 +99,7 @@
 
     def relay_out(i):
         raw_copies[i].wait()
-        return jnp.transpose(raw[i].astype(F32), (1, 0, 2)).astype(BF)
+        return jnp.transpose(raw[i], (1, 0, 2))
 
     pl.semaphore_wait(barrier, len(partners))
 
@@ -211,15 +211,19 @@
     for d in (0, 3, 2, 1):
         qa_zp[d].wait_recv()
         go(qa_fwd[d])
+    def turn_across(d):
+        kv_y[d].wait_recv()
+        k_t[1, :, pl.ds(d * 128, 128)] = jnp.transpose(kv[1, d, pl.ds(128, 128), :].astype(F32)).astype(BF)
+
+    for d in range(4):
+        k_t[0, :, pl.ds(d * 128, 128)] = jnp.transpose(kv[0, d, pl.ds(128, 128), :].astype(F32)).astype(BF)
+    for d in (0, 3, 2):
+        turn_across(d)
     for d in (3, 2, 1):
         late_z[d].wait_recv()
         go(late_zp[d])
         go(late_sib[d])
-    for d in range(4):
-        k_t[0, :, pl.ds(d * 128, 128)] = jnp.transpose(kv[0, d, pl.ds(128, 128), :].astype(F32)).astype(BF)
-    for d in range(4):
-        kv_y[d].wait_recv()
-        k_t[1, :, pl.ds(d * 128, 128)] = jnp.transpose(kv[1, d, pl.ds(128, 128), :].astype(F32)).astype(BF)
+    turn_across(1)
 
     def step(kk, kp, qc, first_k=False, first_q=False):
         keys = [kv[kk, 2 * kp + i, pl.ds(128, 128), :] for i in (0, 1)]
@@ -262,8 +266,6 @@
     for d in (0, 3, 2, 1):
         late_zp[d].wait_recv()
         go(late_fwd[d])
-    step(0, 1, 0, True)
-    step(0, 0, 0, True)
     for d in range(4):
         qa_sib[d].wait_recv()
         late_sib[d].wait_recv()
@@ -283,8 +285,8 @@
             skv[d, pl.ds(128, 128), :] = (dk_acc[1, rows, :] * SCALE).astype(BF)
             go(kv_back[d])
 
-    step(0, 1, 3)
-    step(0, 0, 3)
+    step(0, 1, 3, True)
+    step(0, 0, 3, True)
     sq[0] = (dq_acc[3] * SCALE).astype(BF)
     q_back3 = remote(sq.at[0], rq.at[0], sibling)
     go(q_back3)
@@ -302,6 +304,8 @@
     sq[2] = (dq_acc[1] * SCALE).astype(BF)
     q_back1 = remote(sq.at[2], rq.at[2], sibling)
     go(q_back1)
+    step(0, 1, 0)
+    step(0, 0, 0)
 
     out_kv = [None] + [remote(fkv.at[d], out.at[m, pl.ds(128, 256)], from_z[d]) for d in (1, 2, 3)]
     out_q = [None] + [remote(fq.at[d], out.at[m, pl.ds(0, 128)], from_z[d]) for d in (1, 2, 3)]
@@ -346,7 +350,7 @@
         load.start()
     for (i, _), load, store in zip(outs, loads, stores):
         load.wait()
-        turned[i] = jnp.transpose(held[i].astype(F32), (1, 0, 2)).astype(BF)
+        turned[i] = jnp.transpose(held[i], (1, 0, 2))
         store.start()
     for store in stores:
         store.wait()

time: 51.7 us -> 51.7 us (level)
  no operation moved by 1% of the time
where the time goes in v3:
time: 51.7 us; the launch traced here: 51.6 us
  Pallas kernels  50.9 us (98%)
  between operations  0.64 us (1%)
    pallas_call x1, Pallas kernels, on_device(): pl.pallas_call(kernel, out_shape=jax.ShapeDtypeStruct((4, 384, 128), BF),...  49.1 us
    pallas_call x1, Pallas kernels, on_device(): pl.pallas_call(token_major, out_shape=[jax.ShapeDtypeStruct((128, 4, 128)...  1.8 us

profile of v3, /device:TPU:2, one launch (start us, length us, event | category | flops | bytes accessed | tf_op | source)
XLA Modules:
  0.0 51.6 jit_solution(2289196074268265877)
XLA Ops:
  0.6 49.1 %shard_map.103.blocks = bf16[4,384,128]{2,1,0:T(8,128)(2,1)} custom-call(bf16[128,512]{1,0:T(8,128)(2,1)} %dl.1, bf16[512,4096]{1,0:T(8,128)(2,1)} %w_hbm.1, bf16[128,4,128]{2,1,0:T(4,128)(2,1)} %v_hbm.1, bf16[128,4,128]{2,1,0:T(4,128)(2,1)} %k_hbm.1, bf16[128,4,128]{2,1,0:T(4,128)(2,1)} %q_hbm.1, bf16[128,4,128]{2,1,0:T(4,128)(2,1)} %o_hbm.1, ...), custom_call_target="tpu_custom_call" | custom-call | tf_op jit(solution)/shard_map/pallas_call | solution.py:362
  49.8 1.8 %shard_map.104 = (bf16[128,4,128]{2,1,0:T(4,128)(2,1)}, bf16[128,4,128]{2,1,0:T(4,128)(2,1)}, bf16[128,4,128]{2,1,0:T(4,128)(2,1)}) custom-call(bf16[4,384,128]{2,1,0:T(8,128)(2,1)} %shard_map.103.blocks), custom_call_target="tpu_custom_call" | custom-call | tf_op jit(solution)/shard_map/pallas_call | solution.py:396
